TPU v7x, 128 devices: a whole 4x4x4 slice. The times are simulated.
128 devices in a mesh: frame: 32 (over x, z, y_hi), head: 4 (over y_lo, core).
Axes of the slice: x: 4, y: 4 (y_hi: 2, y_lo: 2; y = y_hi * 2 + y_lo), z: 4, core: 2. Of those that a mesh axis runs over, the one named last changes fastest.
Arguments:
- tokens: bfloat16 [32, 1024, 1280], P('frame', None, 'head')
- norm_gain: float32 [2, 1280], replicated, may hold values from 0.1 to 1.9
- w_qkv: bfloat16 [2, 1280, 3, 1280], P(None, None, None, 'head')
- w_out: bfloat16 [2, 1280, 1280], P(None, None, 'head'), may hold values from -0.5 to 0.5
- out_bias: bfloat16 [2, 1280], P(None, 'head'), may hold values from -3 to 3
Outputs:
- mixed: bfloat16 [32, 1024, 1280], P('frame', None, 'head')
All inputs are finite; a program needn't handle non-finite values.
Results may differ from a plain program's by a relative error of at most 0.014.
Values may be sent and summed in bfloat16 or wider, within the bound.
A program may use at most 128 MiB of HBM per device.

v0:
```python
import jax
import jax.numpy as jnp
from jax import lax
from jax.sharding import PartitionSpec as P

HEAD_DIM = 64
BLOCKS = 2


def broadcast(array, axis, root):
    mine = lax.axis_index(axis) == root
    return lax.psum(jnp.where(mine, array, jnp.zeros_like(array)), axis)


def shifted(block, axis, distance):
    devices = range(lax.axis_size(axis))
    route = [(i - distance, i) for i in devices if i - distance in devices]
    return lax.ppermute(block, axis, route)


def normalize(activations, gain_row):
    widened = activations.astype(jnp.float32)
    average = jnp.mean(widened, axis=-1, keepdims=True)
    variance = jnp.mean((widened - average) ** 2, axis=-1, keepdims=True)
    return ((widened - average) * lax.rsqrt(variance + 1e-05) * gain_row).astype(jnp.bfloat16)


def attend(queries, first_pair, predecessors, heads_here):
    frame_tokens = queries.shape[1]
    block_rows = min(512, frame_tokens)
    block_count = frame_tokens // block_rows
    scale = HEAD_DIM ** (-0.5)

    def one_frame(frame_item):
        query_rows, pair_rows = frame_item
        key_value = jnp.concatenate([first_pair, pair_rows], 0)
        key_rows = key_value[:, 0].reshape(2 * frame_tokens, heads_here, HEAD_DIM)
        value_rows = key_value[:, 1].reshape(2 * frame_tokens, heads_here, HEAD_DIM)
        query_blocks = query_rows.reshape(block_count, block_rows, heads_here, HEAD_DIM)

        def one_block(query_block):
            scores = (
                jnp.einsum(
                    "qhe,khe->hqk", query_block, key_rows, preferred_element_type=jnp.float32
                )
                * scale
            )
            row_max = jnp.max(scores, axis=-1, keepdims=True)
            expo = jnp.exp(scores - row_max)
            weights = (expo / jnp.sum(expo, axis=-1, keepdims=True)).astype(jnp.bfloat16)
            result = jnp.einsum(
                "hqk,khe->qhe", weights, value_rows, preferred_element_type=jnp.float32
            )
            return result.astype(jnp.bfloat16).reshape(block_rows, heads_here * HEAD_DIM)

        return lax.map(one_block, query_blocks).reshape(frame_tokens, heads_here * HEAD_DIM)

    return lax.map(one_frame, (queries, predecessors))


def project_columns(attended, current_cols, weights_cols, bias_cols):
    row_total = attended.shape[0]
    summed = jnp.dot(
        lax.all_gather(attended, "head", axis=1, tiled=True),
        weights_cols,
        preferred_element_type=jnp.float32,
    )
    widened = (
        summed
        + bias_cols.astype(jnp.float32)
        + current_cols.reshape(row_total, -1).astype(jnp.float32)
    )
    return widened.astype(jnp.bfloat16).reshape(current_cols.shape)


def shards(tokens, norm_gain, w_qkv, w_out, out_bias):
    frame_tokens = tokens.shape[1]
    width_local = tokens.shape[2]
    width = w_qkv.shape[1]
    heads_here = width_local // HEAD_DIM
    position = lax.axis_index("frame")
    current_cols = tokens
    frames_here = current_cols.shape[0]
    current_full = None
    for layer in range(BLOCKS):
        current_full = lax.all_gather(current_cols, "head", axis=2, tiled=True)
        normed = normalize(current_full, norm_gain[layer])
        projected = jnp.dot(
            normed.reshape(-1, width),
            w_qkv[layer].reshape(width, 3 * width_local),
            preferred_element_type=jnp.float32,
        )
        projected = projected.astype(jnp.bfloat16).reshape(
            frames_here, frame_tokens, 3, width_local
        )
        queries = projected[:, :, 0]
        key_value = projected[:, :, 1:]
        first_pair = broadcast(key_value[0], "frame", 0)
        incoming = shifted(key_value[-1], "frame", 1)
        leading = jnp.where(position == 0, key_value[0], incoming)
        pieces = [leading[None], key_value[:-1]]
        predecessors = jnp.concatenate(pieces, 0)
        attended = attend(queries, first_pair, predecessors, heads_here).reshape(-1, width_local)
        current_cols = project_columns(attended, current_cols, w_out[layer], out_bias[layer])
        current_full = None
    return current_cols


def solution(mesh):
    placed = (
        P("frame", None, "head"),
        P(),
        P(None, None, None, "head"),
        P(None, None, "head"),
        P(None, "head"),
    )
    return jax.shard_map(
        shards, mesh=mesh, in_specs=placed, out_specs=P("frame", None, "head"), check_vma=False
    )
```

profile of v0, /device:TPU:27, one launch (start us, length us, event | category | flops | bytes accessed | tf_op | source)
XLA Modules:
  0.0 1055.8 jit_solution(13131953549000417230)
XLA Ops:
  8.7 5.0 fusion.100
  13.7 30.7 %all-gather.6.cloned.1.call-done = bf16[1,1024,1280]{1,2,0:T(8,128)(2,1)} async-done(((bf16[1,1024,320]{1,2,0:T(8,128)(2,1)}), bf16[1,1024,1280]{1,2,0:T(8,128)(2,1)}) %all-gather.6.cloned.1.call-update) | async-done | bytes 2621456 | tf_op jit(solution)/shard_map/all_gather | solution.py:86
  47.7 2.8 fusion.73
  50.6 3.7 collective-permute-start
  54.4 30.2 %collective-permute-done = bf16[1024,2,320]{0,2,1:T(8,128)(2,1)} collective-permute-done((bf16[1024,2,320]{0,2,1:T(8,128)(2,1)S(1)}, bf16[1024,2,320]{0,2,1:T(8,128)(2,1)}, u32[]{:S(2)}, u32[]{:S(2)}) %collective-permute-start) | collective-permute-done | bytes 1310752 | tf_op jit(solution)/shard_map/ppermute | solution.py:18
  91.5 318.3 %all-reduce.3.cloned.1.call-done = bf16[1024,2,320]{0,2,1:T(8,128)(2,1)} async-done(((bf16[1024,2,320]{0,2,1:T(8,128)(2,1)}), bf16[1024,2,320]{0,2,1:T(8,128)(2,1)}) %all-reduce.3.cloned.1.call-update) | async-done | bytes 1310736 | tf_op jit(solution)/shard_map/psum | solution.py:12
  412.4 46.0 %while.34 = (s32[]{:T(128)}, bf16[2,512,320]{1,2,0:T(8,128)(2,1)S(1)}, bf16[2,512,5,64]{1,3,2,0:T(8,128)(2,1)}, bf16[2048,5,64]{0,2,1:T(8,128)(2,1)}, bf16[2048,5,64]{0,2,1:T(8,128)(2,1)S(1)}, /*index=5*/s32[]{:T(128)}) while((s32[]{:T(128)}, bf16[2,512,320]{1,2,0:T(8,128)(2,1)S(1)}, bf16[2,512,5,64]{1,3,2,0:T(8,128)(2,1)}, ...), condition=%wide.region_6.7_spmd, body=%wide.region_3.6_spmd.sunk | while | flops 1368557568 | bytes 45896264 | solution.py:56
  412.4 14.2 %fusion.124 = (f32[5,512]{1,0:T(8,128)S(1)}, f32[5,512,2048]{2,1,0:T(8,128)}) fusion(bf16[2048,5,64]{0,2,1:T(8,128)(2,1)} %get-tuple-element.224, bf16[2,512,5,64]{1,3,2,0:T(8,128)(2,1)} %get-tuple-element.223, s32[]{:T(128)} %get-tuple-element.215), kind=kOutput, calls=%fused_computation.96.clone.1 | convolution fusion | flops 686819328 | bytes 22620672 | tf_op jit(solution)/shard_map/while/body/eval_jaxpr/while/body/eval_jaxpr/sub | solution.py:49
  426.7 8.8 fusion.125
  435.5 14.2 %fusion.124 = (f32[5,512]{1,0:T(8,128)S(1)}, f32[5,512,2048]{2,1,0:T(8,128)}) fusion(bf16[2048,5,64]{0,2,1:T(8,128)(2,1)} %get-tuple-element.224, bf16[2,512,5,64]{1,3,2,0:T(8,128)(2,1)} %get-tuple-element.223, s32[]{:T(128)} %get-tuple-element.215), kind=kOutput, calls=%fused_computation.96.clone.1 | convolution fusion | flops 686819328 | bytes 22620672 | tf_op jit(solution)/shard_map/while/body/eval_jaxpr/while/body/eval_jaxpr/sub | solution.py:49
  449.7 8.8 fusion.125
  460.1 66.3 %all-gather.8.cloned.1.call-done = bf16[1024,1280]{0,1:T(8,128)(2,1)} async-done(((bf16[1024,320]{0,1:T(8,128)(2,1)}), bf16[1024,1280]{0,1:T(8,128)(2,1)}) %all-gather.8.cloned.1.call-update) | async-done | bytes 2621456 | tf_op jit(solution)/shard_map/all_gather | solution.py:64
  526.4 3.9 fusion.82
  530.5 34.2 %all-gather.12.cloned.1.call-done = bf16[1024,1280]{0,1:T(8,128)(2,1)} async-done(((bf16[1024,320]{0,1:T(8,128)(2,1)}), bf16[1024,1280]{0,1:T(8,128)(2,1)}) %all-gather.12.cloned.1.call-update) | async-done | bytes 2621456 | tf_op jit(solution)/shard_map/all_gather | solution.py:86
  571.0 3.7 collective-permute-start.1
  574.7 30.1 %collective-permute-done.1 = bf16[1024,2,320]{0,2,1:T(8,128)(2,1)S(1)} collective-permute-done((bf16[1024,2,320]{0,2,1:T(8,128)(2,1)S(1)}, bf16[1024,2,320]{0,2,1:T(8,128)(2,1)S(1)}, u32[]{:S(2)}, u32[]{:S(2)}) %collective-permute-start.1) | collective-permute-done | bytes 1310752 | tf_op jit(solution)/shard_map/ppermute | solution.py:18
  610.3 318.1 %all-reduce.5.cloned.1.call-done = bf16[1024,2,320]{0,2,1:T(8,128)(2,1)} async-done(((bf16[1024,2,320]{0,2,1:T(8,128)(2,1)}), bf16[1024,2,320]{0,2,1:T(8,128)(2,1)}) %all-reduce.5.cloned.1.call-update) | async-done | bytes 1310736 | tf_op jit(solution)/shard_map/psum | solution.py:12
  931.1 46.0 %while.35 = (s32[]{:T(128)}, bf16[2,512,320]{1,2,0:T(8,128)(2,1)S(1)}, bf16[2,512,5,64]{1,3,2,0:T(8,128)(2,1)}, bf16[2048,5,64]{0,2,1:T(8,128)(2,1)}, bf16[2048,5,64]{0,2,1:T(8,128)(2,1)S(1)}, /*index=5*/s32[]{:T(128)}) while((s32[]{:T(128)}, bf16[2,512,320]{1,2,0:T(8,128)(2,1)S(1)}, bf16[2,512,5,64]{1,3,2,0:T(8,128)(2,1)}, ...), condition=%wide.region_13.14_spmd, body=%wide.region_10.13_spmd.sunk | while | flops 1368557568 | bytes 45896264 | solution.py:56
  931.1 14.2 %fusion.129 = (f32[5,512]{1,0:T(8,128)S(1)}, f32[5,512,2048]{2,1,0:T(8,128)}) fusion(bf16[2048,5,64]{0,2,1:T(8,128)(2,1)} %get-tuple-element.242, bf16[2,512,5,64]{1,3,2,0:T(8,128)(2,1)} %get-tuple-element.241, s32[]{:T(128)} %get-tuple-element.233), kind=kOutput, calls=%fused_computation.97.clone.1 | convolution fusion | flops 686819328 | bytes 22620672 | tf_op jit(solution)/shard_map/while/body/eval_jaxpr/while/body/eval_jaxpr/sub | solution.py:49
  945.3 8.8 fusion.130
  954.1 14.2 %fusion.129 = (f32[5,512]{1,0:T(8,128)S(1)}, f32[5,512,2048]{2,1,0:T(8,128)}) fusion(bf16[2048,5,64]{0,2,1:T(8,128)(2,1)} %get-tuple-element.242, bf16[2,512,5,64]{1,3,2,0:T(8,128)(2,1)} %get-tuple-element.241, s32[]{:T(128)} %get-tuple-element.233), kind=kOutput, calls=%fused_computation.97.clone.1 | convolution fusion | flops 686819328 | bytes 22620672 | tf_op jit(solution)/shard_map/while/body/eval_jaxpr/while/body/eval_jaxpr/sub | solution.py:49
  968.3 8.8 fusion.130
  978.1 67.0 %all-gather.10.cloned.1.call-done = bf16[1024,1280]{0,1:T(8,128)(2,1)} async-done(((bf16[1024,320]{0,1:T(8,128)(2,1)}), bf16[1024,1280]{0,1:T(8,128)(2,1)}) %all-gather.10.cloned.1.call-update) | async-done | bytes 2621456 | tf_op jit(solution)/shard_map/all_gather | solution.py:64
  1045.0 3.9 fusion.85
  (61 shorter events, 32.3 us)
Async XLA Ops:
  6.5 37.8 %all-gather.6.cloned.1.call-start = ((), (), s32[]{:S(2)}) async-start(), calls=%async_computation | async-start | bytes 3276800 | tf_op jit(solution)/shard_map/all_gather | solution.py:86
  7.3 402.5 %all-reduce.3.cloned.1.call-start = ((), (), s32[]{:S(2)}) async-start(), calls=%async_computation.1 | async-start | bytes 2621440 | tf_op jit(solution)/shard_map/psum | solution.py:12
  44.4 2.5 copy-start
  44.4 3.3 copy-start.3
  50.6 33.9 %collective-permute-start = (bf16[1024,2,320]{0,2,1:T(8,128)(2,1)S(1)}, bf16[1024,2,320]{0,2,1:T(8,128)(2,1)}, u32[]{:S(2)}, u32[]{:S(2)}) collective-permute-start(bf16[1024,2,320]{0,2,1:T(8,128)(2,1)S(1)} %slice_bitcast_fusion.1), channel_id=1, source_target_pairs={{0,4},{4,8},{8,12},{12,16},{16,20},{20,24},{24,28},{28,32},{32,36}... | collective-permute-start | bytes 3932168 | tf_op jit(solution)/shard_map/ppermute | solution.py:18
  87.1 439.3 %all-gather.8.cloned.1.call-start = ((), (), s32[]{:S(2)}) async-start(), calls=%async_computation.2 | async-start | bytes 3276800 | tf_op jit(solution)/shard_map/all_gather | solution.py:64
  412.4 47.1 %copy-start.7 = (bf16[2,320]{1,0:T(2,128)(2,1)S(1)}, bf16[2,320]{1,0:T(2,128)(2,1)}, u32[]{:S(2)}) copy-start(bf16[2,320]{1,0:T(2,128)(2,1)} %param.13) | copy-start | bytes 3844
  412.4 114.0 %copy-start.4 = (bf16[1,1024,320]{1,2,0:T(8,128)(2,1)S(1)}, bf16[1,1024,320]{1,2,0:T(8,128)(2,1)}, u32[]{:S(2)}) copy-start(bf16[1,1024,320]{1,2,0:T(8,128)(2,1)} %param.9) | copy-start | bytes 1966084
  459.4 105.3 %all-gather.12.cloned.1.call-start = ((), (), s32[]{:S(2)}) async-start(), calls=%async_computation.5 | async-start | bytes 3276800 | tf_op jit(solution)/shard_map/all_gather | solution.py:86
  530.3 37.8 %copy-start.6 = (f32[1280]{0:T(1024)S(1)}, f32[1280]{0:T(1024)}, u32[]{:S(2)}) copy-start(f32[1280]{0:T(1024)} %get-tuple-element.101) | copy-start | bytes 15364
  530.3 398.2 %all-reduce.5.cloned.1.call-start = ((), (), s32[]{:S(2)}) async-start(), calls=%async_computation.3 | async-start | bytes 2621440 | tf_op jit(solution)/shard_map/psum | solution.py:12
  564.8 2.5 copy-start.1
  564.8 3.3 copy-start.2
  571.0 33.8 %collective-permute-start.1 = (bf16[1024,2,320]{0,2,1:T(8,128)(2,1)S(1)}, bf16[1024,2,320]{0,2,1:T(8,128)(2,1)S(1)}, u32[]{:S(2)}, u32[]{:S(2)}) collective-permute-start(bf16[1024,2,320]{0,2,1:T(8,128)(2,1)S(1)} %slice_bitcast_fusion), channel_id=1, source_target_pairs={{0,4},{4,8},{8,12},{12,16},{16,20},{20,24},{24,28},{28,32},{32,36}... | collective-permute-start | bytes 3932168 | tf_op jit(solution)/shard_map/ppermute | solution.py:18
  606.1 438.9 %all-gather.10.cloned.1.call-start = ((), (), s32[]{:S(2)}) async-start(), calls=%async_computation.4 | async-start | bytes 3276800 | tf_op jit(solution)/shard_map/all_gather | solution.py:64
  931.1 114.0 %copy-start.5 = (bf16[1024,320]{0,1:T(8,128)(2,1)S(1)}, bf16[1024,320]{0,1:T(8,128)(2,1)}, u32[]{:S(2)}) copy-start(bf16[1024,320]{0,1:T(8,128)(2,1)} %fusion.82) | copy-start | bytes 1966084
  931.1 114.0 %copy-start.8 = (f32[320]{0:T(512)S(1)}, f32[320]{0:T(512)}, u32[]{:S(2)}) copy-start(f32[320]{0:T(512)} %get-tuple-element.103) | copy-start | bytes 3844
Sparse Core Ops, SparseCore 0:
  9.0 35.3 all-gather.5
  87.2 322.4 all-reduce.2
  459.6 66.7 all-gather.7
  530.4 34.3 all-gather.11
  606.2 322.1 all-reduce.4
  978.2 66.7 all-gather.9
where the time goes:
time: 1060 us
  waiting for transfers between devices  896 us (85%)
  matrix products  105 us (10%)
  local copies, waits for them, and re-layouts  17.3 us (2%)
  other arithmetic  15.8 us (1%)
  between operations  13.6 us (1%)
    psum x2, waiting for transfers between devices, broadcast(): return lax.psum(jnp.where(mine, array, jnp.zeros_like(array)), axis)  636 us
    all_gather x2, waiting for transfers between devices, project_columns(): lax.all_gather(attended, 'head', axis=1, tiled=True)  133 us
    all_gather x2, waiting for transfers between devices, shards(): current_full = lax.all_gather(current_cols, 'head', axis=2, tiled=True)  64.9 us
    ppermute x2, waiting for transfers between devices, shifted(): return lax.ppermute(block, axis, route)  60.3 us
    sub x4, matrix products, one_block(): expo = jnp.exp(scores - row_max)  56.7 us
    dot_general x4, matrix products, one_block(): jnp.einsum('hqk,khe->qhe', weights, value_rows, preferred_element_type=jn...  35.1 us
  transfers between devices with their start and end apart: 8, of which 8 were waited for; matrix products, arithmetic and copies ran while one was open for 1% of the time, Pallas kernels for 0%

commit v1 on v0

v1 whole, which is shorter than its diff:
```python
import functools

import jax
import jax.numpy as jnp
from jax import lax
from jax.experimental import pallas as pl
from jax.experimental.pallas import tpu as pltpu
from jax.sharding import PartitionSpec as P

HEAD_DIM = 64
BLOCKS = 2
HEADS = 5
CHUNKS = 4
RING = 4
MESH = pl.DeviceIdType.MESH
f32 = jnp.float32
bf16 = jnp.bfloat16
SCALE = HEAD_DIM**-0.5 * 1.4426950408889634


def rcopy(src, dst, send, recv, device):
    return pltpu.make_async_remote_copy(
        src_ref=src,
        dst_ref=dst,
        send_sem=send,
        recv_sem=recv,
        device_id=device,
        device_id_type=MESH,
    )


def kernel(
    tok, gain, w, wo, bias, out,
    xg, x1, wbuf, wo0, bo0, wo1, bo1, q_s, kv, kvp, kv0, attg, att1, res, acc_s, m_s, l_s,
    x_send, xf_send, x_recv, w_send, w_recv, o_send, o_recv, b_send, b_recv,
    kv_send, kv_recv, z_send, z_recv, a_send, af_send, a_recv, h_send, h_recv, r_send, r_recv,
):
    tokens = tok.shape[0]
    qw = tok.shape[1]
    width = gain.shape[1]
    cr = tokens // CHUNKS
    f = lax.axis_index("frame")
    h = lax.axis_index("head")
    k, y, c = f // 2, (f % 2) * 2 + h // 2, h % 2
    x, z = k // RING, k % RING
    frames = lax.axis_size("frame")
    frame = 2 * k + c
    home = y // 2
    rel = (y - 2 * c + RING) % RING
    q_own = (y % 2) * 2 + c
    group = (y % 2) * 2 + y // 2

    def dev(kk, yy, cc):
        return (kk * 2 + yy // 2, (yy % 2) * 2 + cc)

    def plane(dx, dz, cc):
        return dev(((x + dx + RING) % RING) * RING + (z + dz + RING) % RING, y, cc)

    yp, ym = (y + 1) % RING, (y + RING - 1) % RING
    other = dev(k, y, 1 - c)
    ks = frames // 2
    far = dev((k + jnp.where(c == 1, 1, ks - 1)) % ks, y, 1 - c)
    target = dev(((frame + 1) % frames) // 2, y, 1 - c)

    barrier = pltpu.get_barrier_semaphore()
    friends = [
        other, far,
        dev(k, yp, 0), dev(k, yp, 1), dev(k, ym, 0), dev(k, ym, 1),
        plane(1, 0, c), plane(-1, 0, c), plane(0, 1, c), plane(0, -1, c),
    ]
    for d in friends:
        pl.semaphore_signal(barrier, inc=1, device_id=d, device_id_type=MESH)
    pl.semaphore_wait(barrier, len(friends))

    def rows(ch):
        return pl.ds(ch * cr if isinstance(ch, int) else pl.multiple_of(ch * cr, cr), cr)

    def x_send_to(i, ch, device):
        r = rows(ch)
        return rcopy(tok.at[r], xg.at[q_own, r], x_send.at[i, ch], x_recv.at[q_own, ch], device)

    def x_wait(q, ch):
        r = rows(ch)
        rcopy(xg.at[q, r], xg.at[q, r], x_send.at[0, 0], x_recv.at[q, ch], other).wait_recv()

    plus = jnp.logical_or(rel == 1, rel == 2)
    fbase = jnp.where(plus, 0, 2)
    fpair = 2 * (1 - rel % 2)
    fdev = dev(k, jnp.where(plus, yp, ym), c)

    def x_fwd(j, s):
        r = rows(fbase + s)
        qq = fpair + j
        return rcopy(xg.at[qq, r], xg.at[qq, r], xf_send.at[j, s], x_recv.at[qq, fbase + s], fdev)

    def x_local(ch):
        r = rows(ch)
        return pltpu.make_async_copy(tok.at[r], xg.at[q_own, r], x_recv.at[q_own, ch])

    def x_issue(s):
        for first, second in ((s, 2 + s),):
            x_send_to(0, first, dev(k, yp, home)).start()
            x_send_to(1, second, dev(k, ym, home)).start()
            x_send_to(0, second, dev(k, yp, home)).start()
            x_send_to(1, first, dev(k, ym, home)).start()

        @pl.when(c == home)
        def _():
            x_local(s).start()
            x_local(2 + s).start()

        @pl.when(c != home)
        def _():
            x_send_to(2, s, other).start()
            x_send_to(2, 2 + s, other).start()

    x_issue(0)
    x_issue(1)

    for layer in range(BLOCKS):
        @pl.when(c == home)
        def _():
            pltpu.make_async_copy(w.at[layer], wbuf.at[layer], w_recv.at[layer]).start()
            rcopy(w.at[layer], wbuf.at[layer], w_send.at[layer], w_recv.at[layer], other).start()

    def w_wait(layer):
        rcopy(wbuf.at[layer], wbuf.at[layer], w_send.at[0], w_recv.at[layer], other).wait_recv()

    def wo1_copies():
        return (
            rcopy(wo.at[1], wo1.at[c], o_send.at[3], o_recv.at[4 + c], other),
            rcopy(bias.at[1], bo1.at[c], b_send.at[3], b_recv.at[4 + c], other),
        )

    @pl.when(c == home)
    def _():
        pltpu.make_async_copy(wo.at[1], wo1.at[c], o_recv.at[4 + c]).start()
        pltpu.make_async_copy(bias.at[1], bo1.at[c], b_recv.at[4 + c]).start()

    @pl.when(c != home)
    def _():
        for cp in wo1_copies():
            cp.start()

    def wo0_send(i, src_w, src_b, q, device):
        return (
            rcopy(src_w, wo0.at[q], o_send.at[i], o_recv.at[q], device),
            rcopy(src_b, bo0.at[q], b_send.at[i], b_recv.at[q], device),
        )

    def wo0_own():
        return (
            wo0_send(0, wo.at[0], bias.at[0], q_own, other)
            + wo0_send(1, wo.at[0], bias.at[0], q_own, dev(k, ym, c))
        )

    q_next = (yp % 2) * 2 + c

    def wo0_fwd():
        return wo0_send(2, wo0.at[q_next], bo0.at[q_next], q_next, other)

    def wo0_wait(q):
        for cp in wo0_send(0, wo0.at[q], bo0.at[q], q, other):
            cp.wait_recv()

    def ln_qkv(layer, src, ch):
        r = rows(ch)
        xs = [src[q, r, :].astype(f32) for q in range(4)]
        mean = sum(jnp.sum(v, -1, keepdims=True) for v in xs) * (1.0 / width)
        ds = [v - mean for v in xs]
        var = sum(jnp.sum(v * v, -1, keepdims=True) for v in ds) * (1.0 / width)
        inv = lax.rsqrt(var + 1e-5)
        normed = [
            (v * inv * gain[layer : layer + 1, q * qw : (q + 1) * qw]).astype(bf16)
            for q, v in enumerate(ds)
        ]
        proj = jnp.dot(jnp.concatenate(normed, axis=1), wbuf[layer], preferred_element_type=f32)
        for s in range(HEADS):
            kv[layer, s, r, :] = proj[:, 128 * s : 128 * (s + 1)].astype(bf16)
        q_s[r, :] = (proj[:, 640:] * SCALE).astype(bf16)

    def kv_copy(layer, ch):
        r = rows(ch)
        return rcopy(
            kv.at[layer, :, r], kvp.at[layer, :, r],
            kv_send.at[layer, ch], kv_recv.at[layer, ch], target,
        )

    def zcopy(layer, ch, i, src, device):
        r = rows(ch)
        return rcopy(
            src.at[layer, :, r], kv0.at[layer, :, r],
            z_send.at[layer, ch, i], z_recv.at[layer, ch], device,
        )

    def z_targets(ch):
        low = ch < 2
        up = plane(0, 1, c), plane(0, -1, c), plane(1, 0, c), plane(-1, 0, c)
        conds = (
            jnp.logical_or(z == 0, jnp.logical_and(z == 1, low)),
            jnp.logical_or(z == 0, jnp.logical_and(z == 3, jnp.logical_not(low))),
            jnp.logical_and(z == 0, jnp.logical_or(x == 0, jnp.logical_and(x == 1, low))),
            jnp.logical_and(
                z == 0, jnp.logical_or(x == 0, jnp.logical_and(x == 3, jnp.logical_not(low)))
            ),
        )
        return [(i, d, cond) for i, (d, cond) in enumerate(zip(up, conds))]

    def z_forward(layer, ch, src, method):
        for i, d, cond in z_targets(ch):
            @pl.when(cond)
            def _():
                getattr(zcopy(layer, ch, i, src, d), method)()

        getattr(zcopy(layer, ch, 4, src, other), method)()

    def send_kv(layer, ch):
        r = rows(ch)

        @pl.when(frame < frames - 1)
        def _():
            kv_copy(layer, ch).start()

        @pl.when(frame == 0)
        def _():
            pltpu.make_async_copy(
                kv.at[layer, :, r], kv0.at[layer, :, r], z_recv.at[layer, ch]
            ).start()
            z_forward(layer, ch, kv, "start")

    def z_wait(layer, ch):
        zcopy(layer, ch, 4, kv0, other).wait_recv()

    def relay(layer):
        @pl.when(jnp.logical_and(c == 0, frame > 0))
        def _():
            def body(i, carry):
                ch = (i % 2) * 2 + i // 2
                z_wait(layer, ch)
                z_forward(layer, ch, kv0, "start")
                return carry

            lax.fori_loop(0, CHUNKS, body, 0)

    def relay_end(layer):
        @pl.when(jnp.logical_or(c == 1, frame == 0))
        def _():
            for ch in range(CHUNKS):
                z_wait(layer, ch)

    lane = lax.broadcasted_iota(jnp.int32, (cr, 128), 1)
    ones = jnp.ones((tokens, 128), bf16)

    def half(head, r, keys, layer):
        p, s = head // 2, head % 2
        qq = q_s[r, 128 * p : 128 * (p + 1)]
        if head < 4:
            qq = jnp.where((lane // 64) == s, qq, jnp.zeros_like(qq))
            ks_, vs_ = 2 * p, 2 * p + 1
        else:
            ks_, vs_ = 4, 4
        scores = lax.dot_general(
            qq, keys[layer, ks_], (((1,), (1,)), ((), ())), preferred_element_type=f32
        )
        values = jnp.concatenate([keys[layer, vs_], ones], axis=1)
        return scores, values

    def part1(layer):
        @pl.when(frame > 0)
        def _():
            for ch in range(CHUNKS):
                kv_copy(layer, ch).wait_recv()

            def body(ch, carry):
                r = rows(ch)
                for head in range(HEADS):
                    scores, values = half(head, r, kvp, layer)
                    top = jnp.max(scores, -1, keepdims=True)
                    e = jnp.exp2(scores - top).astype(bf16)
                    o = jnp.dot(e, values, preferred_element_type=f32)
                    acc_s[head, r, :] = o[:, :128]
                    l_s[head, r, :] = o[:, 128:]
                    m_s[head, r, :] = jnp.broadcast_to(top, (cr, 128))
                return carry

            lax.fori_loop(0, CHUNKS, body, 0)

        @pl.when(frame == 0)
        def _():
            def body(ch, carry):
                r = rows(ch)
                for head in range(HEADS):
                    acc_s[head, r, :] = jnp.zeros((cr, 128), f32)
                    l_s[head, r, :] = jnp.zeros((cr, 128), f32)
                    m_s[head, r, :] = jnp.full((cr, 128), -jnp.inf, f32)
                return carry

            lax.fori_loop(0, CHUNKS, body, 0)

    def part2(layer, ch, store):
        r = rows(ch)
        pieces = []
        for head in range(HEADS):
            scores, values = half(head, r, kv0, layer)
            before = m_s[head, r, :]
            top = jnp.maximum(before, jnp.max(scores, -1, keepdims=True))
            wide = jnp.concatenate([top] * (tokens // 128), axis=1)
            e = jnp.exp2(scores - wide).astype(bf16)
            o = jnp.dot(e, values, preferred_element_type=f32)
            alpha = jnp.exp2(before - top)
            total = l_s[head, r, :] * alpha + o[:, 128:]
            pieces.append((acc_s[head, r, :] * alpha + o[:, :128]) / total)
        store(r, 0, jnp.where(lane < 64, pieces[0], pieces[1]).astype(bf16))
        store(r, 1, jnp.where(lane < 64, pieces[2], pieces[3]).astype(bf16))
        store(r, 2, pieces[4][:, :64].astype(bf16))

    def order(i):
        return (i % 2) * 2 + i // 2

    g_m = (ym % 2) * 2 + ym // 2
    g_p = (yp % 2) * 2 + yp // 2
    g_o = (((y + 2) % RING) % 2) * 2 + ((y + 2) % RING) // 2

    for s in range(2):
        x_wait(fpair, fbase + s)
        x_wait(fpair + 1, fbase + s)
        x_fwd(0, s).start()
        x_fwd(1, s).start()
    for s in range(2):
        x_wait(fpair, 2 - fbase + s)
        x_wait(fpair + 1, 2 - fbase + s)
        for j in range(2):
            x_wait(2 - fpair + j, s)
            x_wait(2 - fpair + j, 2 + s)

    w_wait(0)

    def first(i, carry):
        ch = order(i)
        ln_qkv(0, xg, ch)
        send_kv(0, ch)
        return carry

    lax.fori_loop(0, CHUNKS, first, 0)

    pltpu.make_async_copy(wo.at[0], wo0.at[q_own], o_recv.at[q_own]).start()
    pltpu.make_async_copy(bias.at[0], bo0.at[q_own], b_recv.at[q_own]).start()
    for cp in wo0_own():
        cp.start()

    relay(0)
    part1(0)
    relay_end(0)

    wo0_wait(q_next)
    for cp in wo0_fwd():
        cp.start()

    def a_copy(direction, ch):
        r = rows(ch)
        return rcopy(
            attg.at[group, r], attg.at[group, r], a_send.at[direction, ch],
            a_recv.at[group, ch], dev(k, yp if direction == 0 else ym, c),
        )

    def a_fwd(direction, s):
        ch = s if direction == 0 else 2 + s
        g = g_m if direction == 0 else g_p
        r = rows(ch)
        return rcopy(
            attg.at[g, r], attg.at[g, r], af_send.at[direction, s],
            a_recv.at[g, ch], dev(k, yp if direction == 0 else ym, c),
        )

    def a_wait(g, ch):
        r = rows(ch)
        rcopy(attg.at[g, r], attg.at[g, r], a_send.at[0, 0], a_recv.at[g, ch], other).wait_recv()

    def a_forward(s):
        a_wait(g_m, s)
        a_fwd(0, s).start()
        a_wait(g_p, 2 + s)
        a_fwd(1, s).start()

    def store0(r, p, v):
        attg[group, r, 128 * p : 128 * p + v.shape[1]] = v

    def second0(i, carry):
        ch = order(i)
        part2(0, ch, store0)
        a_copy(0, ch).start()
        a_copy(1, ch).start()

        @pl.when(i == 2)
        def _():
            a_forward(0)

        return carry

    lax.fori_loop(0, CHUNKS, second0, 0)
    wo0_wait(q_own)
    wo0_wait((y % 2) * 2 + 1 - c)
    wo0_wait((yp % 2) * 2 + 1 - c)
    w_wait(1)

    def project(ch):
        r = rows(ch)
        attended = jnp.concatenate([attg[g, r, :] for g in range(4)], axis=1)
        for q in range(4):
            summed = jnp.dot(attended, wo0[q], preferred_element_type=f32)
            x1[q, r, :] = (summed + bo0[q, 0:1, :] + xg[q, r, :].astype(f32)).astype(bf16)
        ln_qkv(1, x1, ch)
        send_kv(1, ch)

    a_forward(1)

    def third(i, carry):
        @pl.when(i % 2 == 0)
        def _():
            s = i // 2
            a_wait(g_m, 2 + s)
            a_wait(g_p, s)
            a_wait(g_o, s)
            a_wait(g_o, 2 + s)

        project(order(i))
        return carry

    lax.fori_loop(0, CHUNKS, third, 0)

    relay(1)
    part1(1)
    relay_end(1)

    at_home = rel < 2
    mate = dev(k, jnp.where(rel == 0, yp, ym), c)
    near = dev(k, jnp.where(rel == 2, ym, yp), c)
    g_near = jnp.where(rel == 0, g_m, g_p)
    g_mate = jnp.where(rel == 0, g_p, g_m)

    def h_copy(ch, device):
        r = rows(ch)
        return rcopy(
            att1.at[group, r], att1.at[group, r], h_send.at[0, ch], h_recv.at[group, ch], device
        )

    def h_fwd(ch):
        r = rows(ch)
        return rcopy(
            att1.at[g_near, r], att1.at[g_near, r], h_send.at[1, ch], h_recv.at[g_near, ch], mate
        )

    def h_wait(g, ch):
        r = rows(ch)
        rcopy(att1.at[g, r], att1.at[g, r], h_send.at[0, 0], h_recv.at[g, ch], other).wait_recv()

    def store1(r, p, v):
        att1[group, r, 128 * p : 128 * p + v.shape[1]] = v

    def second1(i, carry):
        ch = order(i)
        part2(1, ch, store1)

        @pl.when(at_home)
        def _():
            h_copy(ch, mate).start()

        @pl.when(jnp.logical_not(at_home))
        def _():
            h_copy(ch, near).start()

        return carry

    lax.fori_loop(0, CHUNKS, second1, 0)

    def r_copy(ch):
        r = rows(ch)
        return rcopy(res.at[1 - c, r], out.at[r], r_send.at[ch], r_recv.at[ch], other)

    @pl.when(at_home)
    def _():
        for j in range(2):
            rcopy(wo.at[1], wo1.at[j], o_send.at[0], o_recv.at[4 + j], other).wait_recv()
            rcopy(bias.at[1], bo1.at[j], b_send.at[0], b_recv.at[4 + j], other).wait_recv()

        def forward(i, carry):
            ch = order(i)
            h_wait(g_near, ch)
            h_fwd(ch).start()
            return carry

        lax.fori_loop(0, CHUNKS, forward, 0)

        def last(i, carry):
            ch = order(i)
            r = rows(ch)
            h_wait(g_mate, ch)
            h_wait(g_o, ch)
            attended = jnp.concatenate([att1[g, r, :] for g in range(4)], axis=1)
            for j in range(2):
                summed = jnp.dot(attended, wo1[j], preferred_element_type=f32)
                total = summed + bo1[j, 0:1, :] + x1[(y % 2) * 2 + j, r, :].astype(f32)
                res[j, r, :] = total.astype(bf16)
            r_copy(ch).start()
            out[r, :] = res[c, r, :]
            return carry

        lax.fori_loop(0, CHUNKS, last, 0)
        for ch in range(CHUNKS):
            r_copy(ch).wait_send()
            h_copy(ch, mate).wait_send()
            h_fwd(ch).wait_send()

    @pl.when(jnp.logical_not(at_home))
    def _():
        for ch in range(CHUNKS):
            h_copy(ch, near).wait_send()
            r_copy(ch).wait_recv()

    for s in range(2):
        for j in range(2):
            x_fwd(j, s).wait_send()
            a_fwd(j, s).wait_send()
    for ch in range(CHUNKS):
        x_send_to(0, ch, other).wait_send()
        x_send_to(1, ch, other).wait_send()
        a_copy(0, ch).wait_send()
        a_copy(1, ch).wait_send()
    for cp in wo0_own() + wo0_fwd():
        cp.wait_send()

    @pl.when(c == home)
    def _():
        for layer in range(BLOCKS):
            rcopy(w.at[layer], wbuf.at[layer], w_send.at[layer], w_recv.at[layer], other).wait_send()

    @pl.when(c != home)
    def _():
        for cp in wo1_copies():
            cp.wait_send()
        for ch in range(CHUNKS):
            x_send_to(2, ch, other).wait_send()

    for layer in range(BLOCKS):
        @pl.when(frame < frames - 1)
        def _():
            for ch in range(CHUNKS):
                kv_copy(layer, ch).wait_send()

        @pl.when(c == 0)
        def _():
            for ch in range(CHUNKS):
                z_forward(layer, ch, kv0, "wait_send")


def arrange(w_qkv):
    q, kk, v = w_qkv[:, :, 0], w_qkv[:, :, 1], w_qkv[:, :, 2]
    gap = jnp.zeros(q.shape[:2] + (HEAD_DIM,), q.dtype)
    return jnp.concatenate(
        [
            kk[..., :128], v[..., :128], kk[..., 128:256], v[..., 128:256],
            v[..., 256:], kk[..., 256:], q[..., :256], gap, q[..., 256:],
        ],
        axis=-1,
    )


def shards(tokens, norm_gain, w_qkv, w_out, out_bias):
    rows, qw = tokens.shape[1:]
    width = w_qkv.shape[1]
    cols = 1024
    w = arrange(w_qkv)
    bias = jnp.broadcast_to(out_bias.astype(f32)[:, None, :], (BLOCKS, 8, qw))
    any_spec = pl.BlockSpec(memory_space=pl.ANY)
    vmem = pl.BlockSpec(memory_space=pltpu.VMEM)
    dma = pltpu.SemaphoreType.DMA
    result = pl.pallas_call(
        kernel,
        out_shape=jax.ShapeDtypeStruct((rows, qw), bf16),
        in_specs=[any_spec, vmem, any_spec, any_spec, any_spec],
        out_specs=vmem,
        scratch_shapes=[
            pltpu.VMEM((4, rows, qw), bf16),
            pltpu.VMEM((4, rows, qw), bf16),
            pltpu.VMEM((BLOCKS, width, cols), bf16),
            pltpu.VMEM((4, width, qw), bf16),
            pltpu.VMEM((4, 8, qw), f32),
            pltpu.VMEM((2, width, qw), bf16),
            pltpu.VMEM((2, 8, qw), f32),
            pltpu.VMEM((rows, 384), bf16),
            pltpu.VMEM((BLOCKS, HEADS, rows, 128), bf16),
            pltpu.VMEM((BLOCKS, HEADS, rows, 128), bf16),
            pltpu.VMEM((BLOCKS, HEADS, rows, 128), bf16),
            pltpu.VMEM((4, rows, qw), bf16),
            pltpu.VMEM((4, rows, qw), bf16),
            pltpu.VMEM((2, rows, qw), bf16),
            pltpu.VMEM((HEADS, rows, 128), f32),
            pltpu.VMEM((HEADS, rows, 128), f32),
            pltpu.VMEM((HEADS, rows, 128), f32),
            dma((3, CHUNKS)), dma((2, 2)), dma((4, CHUNKS)), dma((2,)), dma((2,)),
            dma((4,)), dma((6,)), dma((4,)), dma((6,)),
            dma((BLOCKS, CHUNKS)), dma((BLOCKS, CHUNKS)),
            dma((BLOCKS, CHUNKS, 5)), dma((BLOCKS, CHUNKS)),
            dma((2, CHUNKS)), dma((2, 2)), dma((4, CHUNKS)),
            dma((2, CHUNKS)), dma((4, CHUNKS)), dma((CHUNKS,)), dma((CHUNKS,)),
        ],
        compiler_params=pltpu.CompilerParams(
            collective_id=0, has_side_effects=True, vmem_limit_bytes=60 << 20
        ),
        name="video_blocks",
    )(tokens[0], norm_gain, w, w_out, bias)
    return result[None]


def solution(mesh):
    placed = (
        P("frame", None, "head"),
        P(),
        P(None, None, None, "head"),
        P(None, None, "head"),
        P(None, "head"),
    )
    return jax.shard_map(
        shards, mesh=mesh, in_specs=placed, out_specs=P("frame", None, "head"), check_vma=False
    )
```

time: 1060 us -> 199 us (0.19)
  the two profiles are of different devices: /device:TPU:27 before, /device:TPU:69 now
where the time goes in v1:
time: 199 us; the launch traced here: 197 us
  Pallas kernels  155 us (78%)
  local copies, waits for them, and re-layouts  42.7 us (21%)
    pallas_call x1, Pallas kernels, shards(): pl.pallas_call(kernel, out_shape=jax.ShapeDtypeStruct((rows, qw), bf16),...  155 us
    unnamed x13, local copies, waits for them, and re-layouts  15 us
    concatenate x1, local copies, waits for them, and re-layouts, arrange(): jnp.concatenate([kk[..., :128], v[..., :128], kk[..., 128:256], v[..., 12...  9.03 us
    slice x1, local copies, waits for them, and re-layouts, arrange(): q, kk, v = (w_qkv[:, :, 0], w_qkv[:, :, 1], w_qkv[:, :, 2])  4.73 us

profile of v1, /device:TPU:69, one launch (start us, length us, event | category | flops | bytes accessed | tf_op | source)
XLA Modules:
  0.0 197.3 jit_solution(8678651983251083104)
XLA Ops:
  0.0 4.7 %fusion = (bf16[2,1280,1,320]{1,3,2,0:T(8,128)(2,1)}, bf16[2,1280,1,320]{1,3,2,0:T(8,128)(2,1)}, bf16[2,1280,1,320]{1,3,2,0:T(8,128)(2,1)}) fusion(bf16[2,1280,3,320]{1,3,2,0:T(8,128)(2,1)} %param.7), kind=kLoop, calls=%fused_computation | loop fusion | bytes 9830400 | tf_op jit(solution)/shard_map/slice | solution.py:557
  4.7 2.7 %copy.12 = bf16[2,1280,1,320]{3,1,0,2:T(8,128)(2,1)S(1)} copy(bf16[2,1280,1,320]{1,3,2,0:T(8,128)(2,1)} %get-tuple-element.7) | data formatting | bytes 3276800
  7.5 1.3 fusion.1
  8.8 3.7 %copy.13 = bf16[2,1280,1,320]{3,1,0,2:T(8,128)(2,1)} copy(bf16[2,1280,1,320]{1,3,2,0:T(8,128)(2,1)} %get-tuple-element.6) | data formatting | bytes 3276800
  12.4 1.4 slice.45
  13.8 3.7 %copy.14 = bf16[2,1280,1,320]{3,1,0,2:T(8,128)(2,1)} copy(bf16[2,1280,1,320]{1,3,2,0:T(8,128)(2,1)} %get-tuple-element.5) | data formatting | bytes 3276800
  17.5 2.5 %slice.47 = bf16[2,1280,256]{2,1,0:T(8,128)(2,1)} slice(bf16[2,1280,320]{2,1,0:T(8,128)(2,1)} %bitcast.9), slice={[0:2], [0:1280], [0:256]} | slice | bytes 2621440 | tf_op jit(solution)/shard_map/slice | solution.py:562
  20.0 2.0 %slice.43 = bf16[2,1280,128]{2,1,0:T(8,128)(2,1)} slice(bf16[2,1280,320]{2,1,0:T(8,128)(2,1)} %bitcast.8), slice={[0:2], [0:1280], [0:128]} | slice | bytes 1310720 | tf_op jit(solution)/shard_map/slice | solution.py:561
  22.0 0.9 slice.46
  22.8 0.0 copy-start
  22.8 0.0 copy-start.1
  22.8 2.1 %slice.48 = bf16[2,1280,64]{2,1,0:T(8,128)(2,1)} slice(bf16[2,1280,320]{2,1,0:T(8,128)(2,1)} %bitcast.10), slice={[0:2], [0:1280], [256:320]} | slice | bytes 655360 | tf_op jit(solution)/shard_map/slice | solution.py:562
  25.0 1.0 broadcast_in_dim.12
  25.9 0.0 copy-done
  25.9 0.0 copy-done.1
  25.9 9.0 %concatenate.3.w = bf16[2,1280,1024]{2,1,0:T(8,128)(2,1)} concatenate(bf16[2,1280,128]{2,1,0:T(8,128)(2,1)} %get-tuple-element.9, bf16[2,1280,128]{2,1,0:T(8,128)(2,1)} %slice.43, bf16[2,1280,128]{2,1,0:T(8,128)(2,1)S(1)} %copy-done.1, bf16[2,1280,192]{2,1,0:T(8,128)(2,1)S(1)} %slice.45, bf16[2,1280,64]{2,1,0:T(8,128)(2,1)} %slice.46, bf16[2,1280,256]{2,1,0:T(8,128)(2,1)S(1)} %copy-done, ...), dimensions={2} | concatenate | bytes 10485760 | tf_op jit(solution)/shard_map/concatenate | solution.py:559
  35.0 0.0 copy-start.2
  35.0 3.8 %copy.10.wo = bf16[2,1280,320]{2,1,0:T(8,128)(2,1)} copy(bf16[2,1280,320]{1,2,0:T(8,128)(2,1)} %param.8) | data formatting | bytes 3276800 | tf_op args[3]
  38.8 0.0 copy-done.2
  38.8 1.2 copy.6
  39.9 0.0 copy-done.3
  39.9 0.6 broadcast_in_dim.13.bias
  40.5 154.5 %video_blocks.1 = bf16[1024,320]{1,0:T(8,128)(2,1)} custom-call(bf16[1024,320]{1,0:T(8,128)(2,1)} %bitcast.12, f32[2,1280]{1,0:T(2,128)} %gain.1, bf16[2,1280,1024]{2,1,0:T(8,128)(2,1)} %concatenate.3.w, bf16[2,1280,320]{2,1,0:T(8,128)(2,1)} %copy.10.wo, f32[2,8,320]{2,1,0:T(8,128)} %broadcast_in_dim.13.bias), custom_call_target="tpu_custom_call" | custom-call | tf_op jit(solution)/shard_map/video_blocks/pallas_call | solution.py:577
  195.1 2.2 %copy.11 = bf16[1,1024,320]{1,2,0:T(8,128)(2,1)} copy(bf16[1,1024,320]{2,1,0:T(8,128)(2,1)} %bitcast.11) | data formatting | bytes 1310720 | tf_op jit(solution)/shard_map/broadcast_in_dim | solution.py:612
  (1 shorter events, 0.0 us)
Async XLA Ops:
  22.8 3.1 %copy-start = (bf16[2,1280,256]{2,1,0:T(8,128)(2,1)S(1)}, bf16[2,1280,256]{2,1,0:T(8,128)(2,1)}, u32[]{:S(2)}) copy-start(bf16[2,1280,256]{2,1,0:T(8,128)(2,1)} %slice.47) | copy-start | bytes 3932164
  22.8 3.1 %copy-start.1 = (bf16[2,1280,128]{2,1,0:T(8,128)(2,1)S(1)}, bf16[2,1280,128]{2,1,0:T(8,128)(2,1)}, u32[]{:S(2)}) copy-start(bf16[2,1280,128]{2,1,0:T(8,128)(2,1)} %get-tuple-element.8) | copy-start | bytes 1966084
  35.0 3.8 %copy-start.2 = (bf16[1,1024,320]{1,2,0:T(8,128)(2,1)S(1)}, bf16[1,1024,320]{1,2,0:T(8,128)(2,1)}, u32[]{:S(2)}) copy-start(bf16[1,1024,320]{1,2,0:T(8,128)(2,1)} %param.5) | copy-start | bytes 1966084
  35.0 4.9 %copy-start.3 = (bf16[2,320]{1,0:T(2,128)(2,1)S(1)}, bf16[2,320]{1,0:T(2,128)(2,1)}, u32[]{:S(2)}) copy-start(bf16[2,320]{1,0:T(2,128)(2,1)} %param.9) | copy-start | bytes 3844

commit v2 on v0

v2 whole, which is shorter than its diff:
```python
import functools

import jax
import jax.numpy as jnp
from jax import lax
from jax.experimental import pallas as pl
from jax.experimental.pallas import tpu as pltpu
from jax.sharding import PartitionSpec as P

HEAD_DIM = 64
BLOCKS = 2
HEADS = 5
CHUNKS = 8
STEPS = 4
HALVES = 2
RING = 4
MESH = pl.DeviceIdType.MESH
f32 = jnp.float32
bf16 = jnp.bfloat16
SCALE = HEAD_DIM**-0.5 * 1.4426950408889634


def rcopy(src, dst, send, recv, device):
    return pltpu.make_async_remote_copy(
        src_ref=src,
        dst_ref=dst,
        send_sem=send,
        recv_sem=recv,
        device_id=device,
        device_id_type=MESH,
    )


def kernel(
    tok, gain, w, wo, bias, out,
    xg, x1, wbuf, wo0, bo0, wo1, bo1, q_s, kv, kvp, kv0, attg, att1, res, acc_s, m_s, l_s, gcol, bcol,
    x_send, xf_send, x_recv, w_send, w_recv, o_send, o_recv, b_send, b_recv,
    kv_send, kv_recv, q_send, q_recv, d_send, z_send, z_recv, t_recv, c_send, c_recv, a_send, af_send, a_recv, h_send, h_recv, r_send, r_recv,
):
    qw, tokens = tok.shape
    width = gain.shape[1]
    cr = tokens // CHUNKS
    step_tokens = tokens // STEPS
    half_tokens = tokens // HALVES
    zr = 2 * qw // RING
    f = lax.axis_index("frame")
    h = lax.axis_index("head")
    k, y, c = f // 2, (f % 2) * 2 + h // 2, h % 2
    x, z = k // RING, k % RING
    frames = lax.axis_size("frame")
    frame = 2 * k + c
    home = y // 2
    rel = (y - 2 * c + RING) % RING

    def quarter(yy, cc):
        return (yy % 2) * 2 + cc

    def group_of(yy):
        return (yy % 2) * 2 + yy // 2

    def dev(kk, yy, cc):
        return (kk * 2 + yy // 2, (yy % 2) * 2 + cc)

    q_own = quarter(y, c)
    group = group_of(y)
    yp, ym, yo = (y + 1) % RING, (y + RING - 1) % RING, (y + 2) % RING
    g_m, g_p, g_o = group_of(ym), group_of(yp), group_of(yo)
    other = dev(k, y, 1 - c)
    ks = frames // 2
    far = dev((k + jnp.where(c == 1, 1, ks - 1)) % ks, y, 1 - c)
    target = dev(((frame + 1) % frames) // 2, y, 1 - c)

    barrier = pltpu.get_barrier_semaphore()
    friends = [
        other, far, dev(k, yo, c),
        dev(k, yp, 0), dev(k, yp, 1), dev(k, ym, 0), dev(k, ym, 1),
    ]
    for d in friends:
        pl.semaphore_signal(barrier, inc=1, device_id=d, device_id_type=MESH)

    def along_x(i):
        return dev((x + i) % RING * RING + z, y, 0)

    def along_z(i):
        return dev(x * RING + (z + i) % RING, y, 0)

    @pl.when(c == 0)
    def _():
        for i in range(1, RING):
            for d in (along_x(i), along_z(i)):
                pl.semaphore_signal(barrier, inc=1, device_id=d, device_id_type=MESH)

    pl.semaphore_wait(barrier, len(friends) + 2 * (RING - 1) * (1 - c))

    def span(i, size):
        return pl.ds(i * size if isinstance(i, int) else pl.multiple_of(i * size, size), size)

    def quart(q, size=None):
        return span(q, qw if size is None else size)

    def x_send_to(i, ch, device):
        t = span(ch, cr)
        return rcopy(
            tok.at[:, t], xg.at[quart(q_own), t], x_send.at[i, ch], x_recv.at[q_own, ch], device
        )

    def x_wait(q, ch):
        part = xg.at[quart(q), span(ch, cr)]
        rcopy(part, part, x_send.at[0, 0], x_recv.at[q, ch], other).wait_recv()

    plus = jnp.logical_or(rel == 1, rel == 2)
    off = jnp.where(plus, 0, 1)
    fpair = 2 * (1 - rel % 2)
    fdev = dev(k, jnp.where(plus, yp, ym), c)

    def x_fwd(j, s):
        part = xg.at[quart(fpair + j), span(2 * s + off, cr)]
        return rcopy(part, part, xf_send.at[j, s], x_recv.at[fpair + j, 2 * s + off], fdev)

    def x_local(ch):
        t = span(ch, cr)
        return pltpu.make_async_copy(tok.at[:, t], xg.at[quart(q_own), t], x_recv.at[q_own, ch])

    def x_issue(s):
        a, b = 2 * s, 2 * s + 1
        x_send_to(0, a, dev(k, yp, home)).start()
        x_send_to(1, b, dev(k, ym, home)).start()
        x_send_to(0, b, dev(k, yp, home)).start()
        x_send_to(1, a, dev(k, ym, home)).start()

        @pl.when(c == home)
        def _():
            x_local(a).start()
            x_local(b).start()

        @pl.when(c != home)
        def _():
            x_send_to(2, a, other).start()
            x_send_to(2, b, other).start()

    def w_local(layer):
        return pltpu.make_async_copy(w.at[layer], wbuf.at[layer], w_recv.at[layer])

    def w_give(layer):
        return rcopy(w.at[layer], wbuf.at[layer], w_send.at[layer], w_recv.at[layer], other)

    def w_wait(layer):
        rcopy(wbuf.at[layer], wbuf.at[layer], w_send.at[0], w_recv.at[layer], other).wait_recv()

    def wo1_copies():
        return (
            rcopy(wo.at[1], wo1.at[c], o_send.at[4], o_recv.at[8 + c], other),
            rcopy(bcol.at[1], bo1.at[c], b_send.at[4], b_recv.at[4 + c], other),
        )

    hw = qw // 2

    def wo0_part(i, src, row, size, recv, device):
        return rcopy(src, wo0.at[pl.ds(row, size)], o_send.at[i], o_recv.at[recv], device)

    def bo0_part(i, src, q, device):
        return rcopy(src, bo0.at[quart(q)], b_send.at[i], b_recv.at[q], device)

    def mult(v):
        return pl.multiple_of(v, 32)

    def wo0_own():
        base = q_own * qw
        return (
            wo0_part(0, wo.at[0], mult(base), qw, 2 * q_own, other),
            wo0_part(1, wo.at[0, pl.ds(0, hw)], mult(base), hw, 2 * q_own, dev(k, ym, c)),
            wo0_part(
                2, wo.at[0, pl.ds(hw, hw)], mult(base + hw), hw, 2 * q_own + 1, dev(k, yp, c)
            ),
            bo0_part(0, bcol.at[0], q_own, other),
            bo0_part(1, bcol.at[0], q_own, dev(k, ym, c)),
        )

    q_next = quarter(yp, c)
    q_last = quarter(yp, 1 - c)

    def wo0_fwd():
        return (
            wo0_part(3, wo0.at[quart(q_next)], mult(q_next * qw), qw, 2 * q_next, other),
            bo0_part(2, bo0.at[quart(q_next)], q_next, other),
        )

    def wo0_wait(q, size, recv):
        part = wo0.at[pl.ds(mult(q * qw), size)]
        rcopy(part, part, o_send.at[0], o_recv.at[recv], other).wait_recv()

    def bo0_wait(q):
        bo0_part(0, bo0.at[quart(q)], q, other).wait_recv()

    def ln_qkv(layer, src, s):
        t = span(s, step_tokens)
        wide = step_tokens // 128
        total = 0.0
        for q in range(4):
            total += jnp.sum(src[quart(q), t].astype(f32), 0, keepdims=True)
        mean = total * (1.0 / width)
        total = 0.0
        for q in range(4):
            d = src[quart(q), t].astype(f32) - mean
            total += jnp.sum(d * d, 0, keepdims=True)
        inv = lax.rsqrt(total * (1.0 / width) + 1e-5)
        normed = []
        for q in range(4):
            g = gcol[layer, quart(q), :]
            d = src[quart(q), t].astype(f32) - mean
            normed.append((d * inv * jnp.concatenate([g] * wide, axis=1)).astype(bf16))
        proj = jnp.dot(
            wbuf[layer], jnp.concatenate(normed, axis=0), preferred_element_type=f32
        )
        kv[layer, :, t] = proj[qw:].astype(bf16)
        for p in range(3):
            rows = proj[128 * p : min(128 * (p + 1), qw)] * SCALE
            if p == 2:
                rows = jnp.concatenate([rows, jnp.zeros_like(rows)], axis=0)
            q_s[t, 128 * p : 128 * (p + 1)] = rows.T.astype(bf16)

    def kv_copy(layer, s):
        t = span(s, step_tokens)
        return rcopy(
            kv.at[layer, :, t], kvp.at[layer, :, t],
            kv_send.at[layer, s], kv_recv.at[layer, s], target,
        )

    corner = jnp.logical_and(c == 0, z == 0)
    inner = jnp.logical_and(c == 0, frame > 0)

    def piece(buf, layer, s, i):
        return buf.at[layer, span(i, zr), span(s, half_tokens)]

    def deal(layer, s, i):
        return rcopy(
            piece(kv, layer, s, i), piece(kv0, layer, s, i),
            q_send.at[layer, s, i], q_recv.at[layer, s], along_x(i),
        )

    def lower(layer, s, i, src):
        return rcopy(
            piece(src, layer, s, x), piece(kv0, layer, s, x),
            d_send.at[layer, s, i], q_recv.at[layer, s], along_z(i),
        )

    def spread(layer, s, i, src):
        return rcopy(
            piece(src, layer, s, x), piece(kv0, layer, s, x),
            z_send.at[layer, s, i], z_recv.at[layer, s, x], along_x(i),
        )

    def piece_wait(layer, s, i, recv):
        part = piece(kv0, layer, s, i)
        rcopy(part, part, q_send.at[layer, s, 0], recv, other).wait_recv()

    def root_copy(layer, s):
        t = span(s, half_tokens)
        return pltpu.make_async_copy(
            kv.at[layer, :, t], kv0.at[layer, :, t], t_recv.at[layer, s]
        )

    def core_copy(layer, s):
        part = kv0.at[layer, :, span(s, half_tokens)]
        return rcopy(part, part, c_send.at[layer, s], c_recv.at[layer, s], other)

    def send_kv(layer, s):
        @pl.when(frame < frames - 1)
        def _():
            kv_copy(layer, s).start()

        @pl.when(jnp.logical_and(frame == 0, s % 2 == 1))
        def _():
            p = s // 2
            for i in range(1, RING):
                deal(layer, p, i).start()
            for i in range(1, RING):
                lower(layer, p, i, kv).start()
            for i in range(1, RING):
                spread(layer, p, i, kv).start()
            root_copy(layer, p).start()

        if layer == 1:
            @pl.when(frame == 0)
            def _():
                t = span(s, step_tokens)
                pltpu.make_async_copy(
                    kv.at[layer, :, t], kvp.at[layer, :, t], kv_recv.at[layer, s]
                ).start()

    def down(layer, s):
        @pl.when(jnp.logical_and(corner, x > 0))
        def _():
            piece_wait(layer, s, x, q_recv.at[layer, s])
            for i in range(1, RING):
                lower(layer, s, i, kv0).start()

    def share(layer, s):
        @pl.when(jnp.logical_and(c == 0, z > 0))
        def _():
            piece_wait(layer, s, x, q_recv.at[layer, s])

        @pl.when(inner)
        def _():
            for i in range(1, RING):
                @pl.when(jnp.logical_or(z > 0, x + i != RING))
                def _():
                    spread(layer, s, i, kv0).start()

    def hand_over(layer, s):
        @pl.when(frame == 0)
        def _():
            root_copy(layer, s).wait()

        @pl.when(inner)
        def _():
            for i in range(1, RING):
                j = (x + i) % RING
                piece_wait(layer, s, j, z_recv.at[layer, s, j])

        @pl.when(c == 0)
        def _():
            core_copy(layer, s).start()

    def first_ready(layer):
        @pl.when(c == 1)
        def _():
            for s in range(HALVES):
                core_copy(layer, s).wait_recv()

    def flash(layer, keys, cols, t, size, first):
        count = tokens if cols is None else half_tokens
        cols = slice(None) if cols is None else cols
        lane = lax.broadcasted_iota(jnp.int32, (size, 128), 1)
        found = []
        for head in range(HEADS):
            p = head // 2
            qq = q_s[t, 128 * p : 128 * (p + 1)]
            if head < 4:
                qq = jnp.where((lane // 64) == head % 2, qq, jnp.zeros_like(qq))
                kk = keys[layer, 128 * p : 128 * (p + 1), cols]
                values = [keys[layer, qw + 128 * p : qw + 128 * (p + 1), cols]]
            else:
                qq = qq[:, :64]
                kk = keys[layer, 256:qw, cols]
                values = [keys[layer, qw + 256 : 2 * qw, cols], jnp.zeros((64, count), bf16)]
            values = jnp.concatenate(values + [jnp.ones((128, count), bf16)], axis=0)
            scores = jnp.dot(qq, kk, preferred_element_type=f32)
            top = jnp.max(scores, -1, keepdims=True)
            wide = top
            if not first:
                before = m_s[head, t, :]
                top = jnp.maximum(before, top)
                wide = jnp.concatenate([top] * (count // 128), axis=1)
            e = jnp.exp2(scores - wide).astype(bf16)
            o = lax.dot_general(e, values, (((1,), (1,)), ((), ())), preferred_element_type=f32)
            acc, total = o[:, :128], o[:, 128:]
            if not first:
                alpha = jnp.exp2(before - top)
                acc = acc_s[head, t, :] * alpha + acc
                total = l_s[head, t, :] * alpha + total
            found.append((acc, total, jnp.broadcast_to(top, (size, 128))))
        return found, lane

    def update(layer, keys, cols, first):
        def body(s, carry):
            t = span(s, half_tokens)
            found, _ = flash(layer, keys, cols, t, half_tokens, first)
            for head, (acc, total, top) in enumerate(found):
                acc_s[head, t, :] = acc
                l_s[head, t, :] = total
                m_s[head, t, :] = top
            return carry

        lax.fori_loop(0, HALVES, body, 0)

    def finish(layer, keys, cols, s, dst):
        t = span(s, step_tokens)
        found, lane = flash(layer, keys, cols, t, step_tokens, False)
        pieces = [acc / total for acc, total, _ in found]
        base = group * qw
        dst[pl.ds(mult(base), 128), t] = jnp.where(lane < 64, pieces[0], pieces[1]).T.astype(bf16)
        dst[pl.ds(mult(base + 128), 128), t] = (
            jnp.where(lane < 64, pieces[2], pieces[3]).T.astype(bf16)
        )
        dst[pl.ds(mult(base + 256), 64), t] = pieces[4].T[:64].astype(bf16)

    def half_cols(part):
        return slice(part * half_tokens, (part + 1) * half_tokens)

    def wait_previous(layer, part):
        for s in range(2 * part, 2 * part + 2):
            kv_copy(layer, s).wait_recv()

    def a_copy(direction, ch):
        part = attg.at[quart(group), span(ch, cr)]
        return rcopy(
            part, part, a_send.at[direction, ch], a_recv.at[group, ch],
            dev(k, yp if direction == 0 else ym, c),
        )

    def a_fwd(direction, s):
        ch = 2 * s + direction
        g = g_m if direction == 0 else g_p
        part = attg.at[quart(g), span(ch, cr)]
        return rcopy(
            part, part, af_send.at[direction, s], a_recv.at[g, ch],
            dev(k, yp if direction == 0 else ym, c),
        )

    def a_wait(g, ch):
        part = attg.at[quart(g), span(ch, cr)]
        rcopy(part, part, a_send.at[0, 0], a_recv.at[g, ch], other).wait_recv()

    def a_forward(s):
        a_wait(g_m, 2 * s)
        a_fwd(0, s).start()
        a_wait(g_p, 2 * s + 1)
        a_fwd(1, s).start()

    at_home = rel < 2
    mate = dev(k, jnp.where(rel == 0, yp, ym), c)
    near = dev(k, jnp.where(rel == 2, ym, yp), c)
    across = dev(k, yo, c)

    def h_copy(i, s, device):
        part = att1.at[quart(group), span(s, step_tokens)]
        return rcopy(part, part, h_send.at[i, s], h_recv.at[group, s], device)

    def h_wait(g, s):
        part = att1.at[quart(g), span(s, step_tokens)]
        rcopy(part, part, h_send.at[0, 0], h_recv.at[g, s], other).wait_recv()

    def r_copy(s):
        t = span(s, step_tokens)
        return rcopy(res.at[1 - c, :, t], out.at[:, t], r_send.at[s], r_recv.at[s], other)

    x_issue(0)
    x_issue(1)

    @pl.when(c == home)
    def _():
        w_local(0).start()
        w_give(0).start()

    def column(row):
        return jnp.broadcast_to(row, (128, row.shape[1])).T

    for layer in range(BLOCKS):
        gcol[layer] = column(gain[layer : layer + 1, :])
        row = bias[layer : layer + 1, :].astype(f32)
        row = jnp.concatenate([row, jnp.zeros((1, 384 - qw), f32)], axis=1)
        bcol[layer] = column(row)[:qw]

    def first(s, carry):
        x_wait(fpair, 2 * s + off)
        x_wait(fpair + 1, 2 * s + off)
        x_fwd(0, s).start()
        x_fwd(1, s).start()

        @pl.when(s < STEPS - 2)
        def _():
            x_issue(s + 2)

        @pl.when(s == 2)
        def _():
            down(0, 0)

        @pl.when(s == 3)
        def _():
            share(0, 0)

        x_wait(fpair, 2 * s + 1 - off)
        x_wait(fpair + 1, 2 * s + 1 - off)
        for j in range(2):
            x_wait(2 - fpair + j, 2 * s)
            x_wait(2 - fpair + j, 2 * s + 1)

        @pl.when(s == 0)
        def _():
            w_wait(0)

        ln_qkv(0, xg, s)
        send_kv(0, s)

        return carry

    lax.fori_loop(0, STEPS, first, 0)

    @pl.when(c == home)
    def _():
        w_local(1).start()
        w_give(1).start()
        pltpu.make_async_copy(wo.at[1], wo1.at[c], o_recv.at[8 + c]).start()
        pltpu.make_async_copy(bcol.at[1], bo1.at[c], b_recv.at[4 + c]).start()

    @pl.when(c != home)
    def _():
        for cp in wo1_copies():
            cp.start()

    pltpu.make_async_copy(wo.at[0], wo0.at[quart(q_own)], o_recv.at[2 * q_own]).start()
    pltpu.make_async_copy(bcol.at[0], bo0.at[quart(q_own)], b_recv.at[q_own]).start()
    for cp in wo0_own():
        cp.start()

    down(0, 1)

    @pl.when(frame > 0)
    def _():
        wait_previous(0, 0)
        update(0, kvp, half_cols(0), True)

    @pl.when(frame == 0)
    def _():
        acc_s[...] = jnp.zeros(acc_s.shape, f32)
        l_s[...] = jnp.zeros(l_s.shape, f32)
        m_s[...] = jnp.full(m_s.shape, -jnp.inf, f32)

    share(0, 1)
    hand_over(0, 0)

    @pl.when(frame > 0)
    def _():
        wait_previous(0, 1)
        update(0, kvp, half_cols(1), False)

    hand_over(0, 1)
    first_ready(0)

    def second0(s, carry):
        finish(0, kv0, None, s, attg)
        a_copy(0, 2 * s).start()
        a_copy(1, 2 * s + 1).start()
        a_copy(0, 2 * s + 1).start()
        a_copy(1, 2 * s).start()

        @pl.when(s == 0)
        def _():
            wo0_wait(q_next, hw, 2 * q_next)
            wo0_wait(q_next, hw, 2 * q_next + 1)
            bo0_wait(q_next)
            for cp in wo0_fwd():
                cp.start()

        @pl.when(s >= 2)
        def _():
            a_forward(s - 2)

        return carry

    lax.fori_loop(0, STEPS, second0, 0)
    for q in (q_own, quarter(y, 1 - c), q_last):
        wo0_wait(q, qw, 2 * q)
        bo0_wait(q)
    w_wait(1)

    def third(s, carry):
        @pl.when(s < STEPS - 2)
        def _():
            a_forward(s + 2)

        a_wait(g_m, 2 * s + 1)
        a_wait(g_p, 2 * s)
        a_wait(g_o, 2 * s)
        a_wait(g_o, 2 * s + 1)
        t = span(s, step_tokens)
        for q in range(4):
            summed = jnp.dot(wo0[quart(q), :], attg[:, t], preferred_element_type=f32)
            b = jnp.concatenate([bo0[quart(q), :]] * (step_tokens // 128), axis=1)
            x1[quart(q), t] = (summed + b + xg[quart(q), t].astype(f32)).astype(bf16)
        ln_qkv(1, x1, s)
        send_kv(1, s)

        @pl.when(s == 0)
        def _():
            down(1, 0)

        @pl.when(s == 1)
        def _():
            share(1, 0)
            down(1, 1)

        @pl.when(s == 2)
        def _():
            share(1, 1)
            hand_over(1, 0)

        return carry

    lax.fori_loop(0, STEPS, third, 0)

    hand_over(1, 1)
    wait_previous(1, 0)
    update(1, kvp, half_cols(0), True)
    first_ready(1)
    update(1, kv0, None, False)
    wait_previous(1, 1)

    def second1(s, carry):
        finish(1, kvp, half_cols(1), s, att1)

        @pl.when(at_home)
        def _():
            h_copy(0, s, mate).start()

        @pl.when(jnp.logical_not(at_home))
        def _():
            h_copy(0, s, near).start()
            h_copy(1, s, across).start()

        return carry

    lax.fori_loop(0, STEPS, second1, 0)

    @pl.when(at_home)
    def _():
        for j in range(2):
            rcopy(wo.at[1], wo1.at[j], o_send.at[0], o_recv.at[8 + j], other).wait_recv()
            rcopy(bcol.at[1], bo1.at[j], b_send.at[0], b_recv.at[4 + j], other).wait_recv()

        def last(s, carry):
            t = span(s, step_tokens)
            for g in (g_m, g_p, g_o):
                h_wait(g, s)
            for j in range(2):
                summed = jnp.dot(wo1[j], att1[:, t], preferred_element_type=f32)
                b = jnp.concatenate([bo1[j]] * (step_tokens // 128), axis=1)
                before = x1[quart((y % 2) * 2 + j), t].astype(f32)
                res[j, :, t] = (summed + b + before).astype(bf16)
            r_copy(s).start()
            out[:, t] = res[c, :, t]
            return carry

        lax.fori_loop(0, STEPS, last, 0)
        for s in range(STEPS):
            r_copy(s).wait_send()
            h_copy(0, s, mate).wait_send()

    @pl.when(jnp.logical_not(at_home))
    def _():
        for s in range(STEPS):
            h_copy(0, s, near).wait_send()
            h_copy(1, s, across).wait_send()
            r_copy(s).wait_recv()

    for s in range(STEPS):
        for j in range(2):
            x_fwd(j, s).wait_send()
            a_fwd(j, s).wait_send()
    for ch in range(CHUNKS):
        x_send_to(0, ch, other).wait_send()
        x_send_to(1, ch, other).wait_send()
        a_copy(0, ch).wait_send()
        a_copy(1, ch).wait_send()
    for cp in wo0_own() + wo0_fwd():
        cp.wait_send()

    @pl.when(c == home)
    def _():
        for layer in range(BLOCKS):
            w_give(layer).wait_send()

    @pl.when(c != home)
    def _():
        for cp in wo1_copies():
            cp.wait_send()
        for ch in range(CHUNKS):
            x_send_to(2, ch, other).wait_send()

    for layer in range(BLOCKS):
        @pl.when(frame < frames - 1)
        def _():
            for s in range(STEPS):
                kv_copy(layer, s).wait_send()

        for s in range(HALVES):
            @pl.when(corner)
            def _():
                for i in range(1, RING):
                    lower(layer, s, i, kv0).wait_send()

            @pl.when(c == 0)
            def _():
                core_copy(layer, s).wait_send()
                for i in range(1, RING):
                    @pl.when(jnp.logical_or(k == 0, jnp.logical_or(z > 0, x + i != RING)))
                    def _():
                        spread(layer, s, i, kv0).wait_send()

            @pl.when(frame == 0)
            def _():
                for i in range(1, RING):
                    deal(layer, s, i).wait_send()


def shards(tokens, norm_gain, w_qkv, w_out, out_bias):
    rows, qw = tokens.shape[1:]
    width = w_qkv.shape[1]
    w = jnp.transpose(w_qkv, (0, 2, 3, 1)).reshape(BLOCKS, 3 * qw, width)
    wo = jnp.swapaxes(w_out, 1, 2)
    any_spec = pl.BlockSpec(memory_space=pl.ANY)
    vmem = pl.BlockSpec(memory_space=pltpu.VMEM)
    dma = pltpu.SemaphoreType.DMA
    result = pl.pallas_call(
        kernel,
        out_shape=jax.ShapeDtypeStruct((qw, rows), bf16),
        in_specs=[any_spec, vmem, any_spec, any_spec, vmem],
        out_specs=vmem,
        scratch_shapes=[
            pltpu.VMEM((width, rows), bf16),
            pltpu.VMEM((width, rows), bf16),
            pltpu.VMEM((BLOCKS, 3 * qw, width), bf16),
            pltpu.VMEM((width, width), bf16),
            pltpu.VMEM((width, 128), f32),
            pltpu.VMEM((2, qw, width), bf16),
            pltpu.VMEM((2, qw, 128), f32),
            pltpu.VMEM((rows, 384), bf16),
            pltpu.VMEM((BLOCKS, 2 * qw, rows), bf16),
            pltpu.VMEM((BLOCKS, 2 * qw, rows), bf16),
            pltpu.VMEM((BLOCKS, 2 * qw, rows), bf16),
            pltpu.VMEM((width, rows), bf16),
            pltpu.VMEM((width, rows), bf16),
            pltpu.VMEM((2, qw, rows), bf16),
            pltpu.VMEM((HEADS, rows, 128), f32),
            pltpu.VMEM((HEADS, rows, 128), f32),
            pltpu.VMEM((HEADS, rows, 128), f32),
            pltpu.VMEM((BLOCKS, width, 128), f32),
            pltpu.VMEM((BLOCKS, qw, 128), f32),
            dma((3, CHUNKS)), dma((2, STEPS)), dma((4, CHUNKS)), dma((2,)), dma((2,)),
            dma((5,)), dma((10,)), dma((5,)), dma((6,)),
            dma((BLOCKS, STEPS)), dma((BLOCKS, STEPS)),
            dma((BLOCKS, HALVES, 4)), dma((BLOCKS, HALVES)), dma((BLOCKS, HALVES, 4)),
            dma((BLOCKS, HALVES, 4)), dma((BLOCKS, HALVES, 4)),
            dma((BLOCKS, HALVES)), dma((BLOCKS, HALVES)), dma((BLOCKS, HALVES)),
            dma((2, CHUNKS)), dma((2, STEPS)), dma((4, CHUNKS)),
            dma((2, STEPS)), dma((4, STEPS)), dma((STEPS,)), dma((STEPS,)),
        ],
        compiler_params=pltpu.CompilerParams(
            collective_id=0, has_side_effects=True, vmem_limit_bytes=60 << 20
        ),
        name="video_blocks",
    )(jnp.swapaxes(tokens[0], 0, 1), norm_gain, w, wo, out_bias)
    return jnp.swapaxes(result, 0, 1)[None]


def solution(mesh):
    placed = (
        P("frame", None, "head"),
        P(),
        P(None, None, None, "head"),
        P(None, None, "head"),
        P(None, "head"),
    )
    return jax.shard_map(
        shards, mesh=mesh, in_specs=placed, out_specs=P("frame", None, "head"), check_vma=False
    )
```

time: 1060 us -> 133 us (0.13)
  the two profiles are of different devices: /device:TPU:27 before, /device:TPU:65 now
where the time goes in v2:
time: 133 us
  Pallas kernels  131 us (98%)
  local copies, waits for them, and re-layouts  1.97 us (1%)
    pallas_call x1, Pallas kernels, shards(): pl.pallas_call(kernel, out_shape=jax.ShapeDtypeStruct((qw, rows), bf16),...  131 us

profile of v2, /device:TPU:65, one launch (start us, length us, event | category | flops | bytes accessed | tf_op | source)
XLA Modules:
  0.0 133.0 jit_solution(9404517286198188019)
XLA Ops:
  0.0 131.0 %video_blocks.1 = bf16[320,1024]{1,0:T(8,128)(2,1)} custom-call(bf16[320,1024]{1,0:T(8,128)(2,1)} %bitcast.13, f32[2,1280]{1,0:T(2,128)} %gain.1, bf16[2,960,1280]{2,1,0:T(8,128)(2,1)} %bitcast.10, bf16[2,320,1280]{2,1,0:T(8,128)(2,1)} %bitcast.12, bf16[2,320]{1,0:T(2,128)(2,1)} %bias.1), custom_call_target="tpu_custom_call" | custom-call | tf_op jit(solution)/shard_map/video_blocks/pallas_call | solution.py:705
  131.0 2.0 %copy.7 = bf16[1,1024,320]{1,2,0:T(8,128)(2,1)} copy(bf16[1,1024,320]{1,2,0:T(8,128)(2,1)} %bitcast.11) | data formatting | bytes 1310720

commit v3 on v2

--- a/solution.py
+++ b/solution.py
@@ -230,7 +230,7 @@
     inner = jnp.logical_and(c == 0, frame > 0)
 
     def piece(buf, layer, s, i):
-        return buf.at[layer, span(i, zr), span(s, half_tokens)]
+        return buf.at[layer, span(i, zr), span(s, step_tokens)]
 
     def deal(layer, s, i):
         return rcopy(
@@ -255,13 +255,13 @@
         rcopy(part, part, q_send.at[layer, s, 0], recv, other).wait_recv()
 
     def root_copy(layer, s):
-        t = span(s, half_tokens)
+        t = span(s, step_tokens)
         return pltpu.make_async_copy(
             kv.at[layer, :, t], kv0.at[layer, :, t], t_recv.at[layer, s]
         )
 
     def core_copy(layer, s):
-        part = kv0.at[layer, :, span(s, half_tokens)]
+        part = kv0.at[layer, :, span(s, step_tokens)]
         return rcopy(part, part, c_send.at[layer, s], c_recv.at[layer, s], other)
 
     def send_kv(layer, s):
@@ -269,16 +269,15 @@
         def _():
             kv_copy(layer, s).start()
 
-        @pl.when(jnp.logical_and(frame == 0, s % 2 == 1))
-        def _():
-            p = s // 2
+        @pl.when(frame == 0)
+        def _():
             for i in range(1, RING):
-                deal(layer, p, i).start()
+                deal(layer, s, i).start()
             for i in range(1, RING):
-                lower(layer, p, i, kv).start()
+                lower(layer, s, i, kv).start()
             for i in range(1, RING):
-                spread(layer, p, i, kv).start()
-            root_copy(layer, p).start()
+                spread(layer, s, i, kv).start()
+            root_copy(layer, s).start()
 
         if layer == 1:
             @pl.when(frame == 0)
@@ -325,7 +324,7 @@
     def first_ready(layer):
         @pl.when(c == 1)
         def _():
-            for s in range(HALVES):
+            for s in range(STEPS):
                 core_copy(layer, s).wait_recv()
 
     def flash(layer, keys, cols, t, size, first):
@@ -362,17 +361,21 @@
             found.append((acc, total, jnp.broadcast_to(top, (size, 128))))
         return found, lane
 
-    def update(layer, keys, cols, first):
+    def update(layer, keys, cols, first, between=None):
+        size = half_tokens if between is not None else tokens
+
         def body(s, carry):
-            t = span(s, half_tokens)
-            found, _ = flash(layer, keys, cols, t, half_tokens, first)
+            t = span(s, size)
+            found, _ = flash(layer, keys, cols, t, size, first)
             for head, (acc, total, top) in enumerate(found):
                 acc_s[head, t, :] = acc
                 l_s[head, t, :] = total
                 m_s[head, t, :] = top
+            if between is not None:
+                pl.when(s == 0)(between)
             return carry
 
-        lax.fori_loop(0, HALVES, body, 0)
+        lax.fori_loop(0, tokens // size, body, 0)
 
     def finish(layer, keys, cols, s, dst):
         t = span(s, step_tokens)
@@ -462,13 +465,20 @@
         def _():
             x_issue(s + 2)
 
-        @pl.when(s == 2)
-        def _():
-            down(0, 0)
+        @pl.when(s > 0)
+        def _():
+            down(0, s - 1)
+
+        @pl.when(s > 1)
+        def _():
+            share(0, s - 2)
 
         @pl.when(s == 3)
         def _():
-            share(0, 0)
+            pltpu.make_async_copy(wo.at[0], wo0.at[quart(q_own)], o_recv.at[2 * q_own]).start()
+            pltpu.make_async_copy(bcol.at[0], bo0.at[quart(q_own)], b_recv.at[q_own]).start()
+            for cp in wo0_own():
+                cp.start()
 
         x_wait(fpair, 2 * s + 1 - off)
         x_wait(fpair + 1, 2 * s + 1 - off)
@@ -499,17 +509,20 @@
         for cp in wo1_copies():
             cp.start()
 
-    pltpu.make_async_copy(wo.at[0], wo0.at[quart(q_own)], o_recv.at[2 * q_own]).start()
-    pltpu.make_async_copy(bcol.at[0], bo0.at[quart(q_own)], b_recv.at[q_own]).start()
-    for cp in wo0_own():
-        cp.start()
-
-    down(0, 1)
+    def pass_on():
+        wo0_wait(q_next, hw, 2 * q_next)
+        wo0_wait(q_next, hw, 2 * q_next + 1)
+        bo0_wait(q_next)
+        for cp in wo0_fwd():
+            cp.start()
+
+    share(0, 2)
 
     @pl.when(frame > 0)
     def _():
         wait_previous(0, 0)
-        update(0, kvp, half_cols(0), True)
+        update(0, kvp, half_cols(0), True, lambda: down(0, 3))
+        pass_on()
 
     @pl.when(frame == 0)
     def _():
@@ -517,15 +530,15 @@
         l_s[...] = jnp.zeros(l_s.shape, f32)
         m_s[...] = jnp.full(m_s.shape, -jnp.inf, f32)
 
-    share(0, 1)
-    hand_over(0, 0)
+    share(0, 3)
 
     @pl.when(frame > 0)
     def _():
         wait_previous(0, 1)
         update(0, kvp, half_cols(1), False)
 
-    hand_over(0, 1)
+    for s in range(STEPS):
+        hand_over(0, s)
     first_ready(0)
 
     def second0(s, carry):
@@ -535,13 +548,9 @@
         a_copy(0, 2 * s + 1).start()
         a_copy(1, 2 * s).start()
 
-        @pl.when(s == 0)
-        def _():
-            wo0_wait(q_next, hw, 2 * q_next)
-            wo0_wait(q_next, hw, 2 * q_next + 1)
-            bo0_wait(q_next)
-            for cp in wo0_fwd():
-                cp.start()
+        @pl.when(jnp.logical_and(frame == 0, s == 1))
+        def _():
+            pass_on()
 
         @pl.when(s >= 2)
         def _():
@@ -572,27 +581,21 @@
         ln_qkv(1, x1, s)
         send_kv(1, s)
 
-        @pl.when(s == 0)
-        def _():
-            down(1, 0)
-
-        @pl.when(s == 1)
-        def _():
-            share(1, 0)
-            down(1, 1)
-
-        @pl.when(s == 2)
-        def _():
-            share(1, 1)
-            hand_over(1, 0)
+        down(1, s)
+
+        @pl.when(s > 0)
+        def _():
+            share(1, s - 1)
 
         return carry
 
     lax.fori_loop(0, STEPS, third, 0)
 
-    hand_over(1, 1)
+    share(1, 3)
     wait_previous(1, 0)
     update(1, kvp, half_cols(0), True)
+    for s in range(STEPS):
+        hand_over(1, s)
     first_ready(1)
     update(1, kv0, None, False)
     wait_previous(1, 1)
@@ -674,7 +677,7 @@
             for s in range(STEPS):
                 kv_copy(layer, s).wait_send()
 
-        for s in range(HALVES):
+        for s in range(STEPS):
             @pl.when(corner)
             def _():
                 for i in range(1, RING):
@@ -730,9 +733,9 @@
             dma((3, CHUNKS)), dma((2, STEPS)), dma((4, CHUNKS)), dma((2,)), dma((2,)),
             dma((5,)), dma((10,)), dma((5,)), dma((6,)),
             dma((BLOCKS, STEPS)), dma((BLOCKS, STEPS)),
-            dma((BLOCKS, HALVES, 4)), dma((BLOCKS, HALVES)), dma((BLOCKS, HALVES, 4)),
-            dma((BLOCKS, HALVES, 4)), dma((BLOCKS, HALVES, 4)),
-            dma((BLOCKS, HALVES)), dma((BLOCKS, HALVES)), dma((BLOCKS, HALVES)),
+            dma((BLOCKS, STEPS, 4)), dma((BLOCKS, STEPS)), dma((BLOCKS, STEPS, 4)),
+            dma((BLOCKS, STEPS, 4)), dma((BLOCKS, STEPS, 4)),
+            dma((BLOCKS, STEPS)), dma((BLOCKS, STEPS)), dma((BLOCKS, STEPS)),
             dma((2, CHUNKS)), dma((2, STEPS)), dma((4, CHUNKS)),
             dma((2, STEPS)), dma((4, STEPS)), dma((STEPS,)), dma((STEPS,)),
         ],

time: 133 us -> 126 us (0.947)
  the two profiles are of different devices: /device:TPU:65 before, /device:TPU:27 now
where the time goes in v3:
time: 126 us; the launch traced here: 125 us
  Pallas kernels  123 us (98%)
  local copies, waits for them, and re-layouts  1.97 us (2%)
    pallas_call x1, Pallas kernels, shards(): pl.pallas_call(kernel, out_shape=jax.ShapeDtypeStruct((qw, rows), bf16),...  123 us

profile of v3, /device:TPU:27, one launch (start us, length us, event | category | flops | bytes accessed | tf_op | source)
XLA Modules:
  0.0 125.5 jit_solution(1253848751604650530)
XLA Ops:
  0.0 123.5 %video_blocks.1 = bf16[320,1024]{1,0:T(8,128)(2,1)} custom-call(bf16[320,1024]{1,0:T(8,128)(2,1)} %bitcast.13, f32[2,1280]{1,0:T(2,128)} %gain.1, bf16[2,960,1280]{2,1,0:T(8,128)(2,1)} %bitcast.10, bf16[2,320,1280]{2,1,0:T(8,128)(2,1)} %bitcast.12, bf16[2,320]{1,0:T(2,128)(2,1)} %bias.1), custom_call_target="tpu_custom_call" | custom-call | tf_op jit(solution)/shard_map/video_blocks/pallas_call | solution.py:708
  123.5 2.0 %copy.7 = bf16[1,1024,320]{1,2,0:T(8,128)(2,1)} copy(bf16[1,1024,320]{1,2,0:T(8,128)(2,1)} %bitcast.11) | data formatting | bytes 1310720

commit v4 on v3

--- a/solution.py
+++ b/solution.py
@@ -565,10 +565,6 @@
     w_wait(1)
 
     def third(s, carry):
-        @pl.when(s < STEPS - 2)
-        def _():
-            a_forward(s + 2)
-
         a_wait(g_m, 2 * s + 1)
         a_wait(g_p, 2 * s)
         a_wait(g_o, 2 * s)
@@ -578,6 +574,10 @@
             summed = jnp.dot(wo0[quart(q), :], attg[:, t], preferred_element_type=f32)
             b = jnp.concatenate([bo0[quart(q), :]] * (step_tokens // 128), axis=1)
             x1[quart(q), t] = (summed + b + xg[quart(q), t].astype(f32)).astype(bf16)
+        @pl.when(s < STEPS - 2)
+        def _():
+            a_forward(s + 2)
+
         ln_qkv(1, x1, s)
         send_kv(1, s)
 

time: 126 us -> 126 us (level)
  no operation moved by 1% of the time
where the time goes in v4:
time: 126 us; the launch traced here: 125 us
  Pallas kernels  123 us (98%)
  local copies, waits for them, and re-layouts  1.97 us (2%)
    pallas_call x1, Pallas kernels, shards(): pl.pallas_call(kernel, out_shape=jax.ShapeDtypeStruct((qw, rows), bf16),...  123 us

profile of v4, /device:TPU:27, one launch (start us, length us, event | category | flops | bytes accessed | tf_op | source)
XLA Modules:
  0.0 125.4 jit_solution(11255034922252387565)
XLA Ops:
  0.0 123.5 %video_blocks.1 = bf16[320,1024]{1,0:T(8,128)(2,1)} custom-call(bf16[320,1024]{1,0:T(8,128)(2,1)} %bitcast.13, f32[2,1280]{1,0:T(2,128)} %gain.1, bf16[2,960,1280]{2,1,0:T(8,128)(2,1)} %bitcast.10, bf16[2,320,1280]{2,1,0:T(8,128)(2,1)} %bitcast.12, bf16[2,320]{1,0:T(2,128)(2,1)} %bias.1), custom_call_target="tpu_custom_call" | custom-call | tf_op jit(solution)/shard_map/video_blocks/pallas_call | solution.py:708
  123.5 2.0 %copy.7 = bf16[1,1024,320]{1,2,0:T(8,128)(2,1)} copy(bf16[1,1024,320]{1,2,0:T(8,128)(2,1)} %bitcast.11) | data formatting | bytes 1310720
